TPU v7x, 32 devices: a whole 2x2x4 slice. The times are simulated.
32 devices in a mesh: seq: 8 (over z, y), tp: 4 (over x, core).
Axes of the slice: x: 2, y: 2, z: 4, core: 2. Of those that a mesh axis runs over, the one named last changes fastest.
Arguments:
- tokens: bfloat16 [2048, 1280], P('seq'), may hold values from -45 to 45
- ln_gain: float32 [1280], replicated, may hold values from 0.6 to 10, as said below
- ln_bias: float32 [1280], replicated, may hold values from -3 to 3
- w_qkv: bfloat16 [3, 1280, 1280], P(None, None, 'tp'), may hold values from -0.15625 to 0.15625
- b_qkv: float32 [3, 1280], P(None, 'tp'), may hold values from -3 to 3
- w_out: bfloat16 [1280, 1280], P('tp'), may hold values from -0.15625 to 0.15625
- b_out: float32 [1280], replicated, may hold values from -3 to 3
- merge_gain: float32 [1280], replicated, may hold values from 0.25 to 1.75
- merge_bias: float32 [1280], replicated, may hold values from -3 to 3
- segments: int32 [512], replicated, may hold values from 0 to 3, never falling along the last dimension, each value on 1 to 256 neighbouring positions
- owners: int32 [512, 1], P('seq'), may hold values from 0 to 7; in each aligned block of 64 rows (0 to 63, 64 to 127, ...) at most 16 rows name the same one
Outputs:
- routed: bfloat16 [1024, 5120], P('seq', 'tp')
Inputs may be any that keep to these rules, and one draw needn't show every extreme that they name: `segments`: Non-decreasing along the rows; one image holds at most 256 merged rows, and some image holds exactly that many. `owners`: among the 64 merged rows of one device no owner is named more than 16 times, a bound that some block reaches. `ln_gain`: gains are positive, within 0.6 to 10.
All inputs are finite; a program needn't handle non-finite values.
Results may differ from a plain program's by a relative error of at most 0.024.
The roundings to bfloat16 on the way count: a program that leaves them out, or rounds other values in their place, can miss the bound.
Values may be sent and summed in bfloat16 or wider, within the bound.
A program may use at most 64 MiB of HBM per device.

v0:
```python
import jax
import jax.numpy as jnp
from jax import lax
from jax.sharding import PartitionSpec as P

HEAD_DIM = 80
SPAN = 4


epsilon = 1e-06
masked_score = -1e30


def from_behind(value, axis, steps):
    count = lax.axis_size(axis)
    leading, last = (max(0, -steps), min(count, count - steps))
    return lax.ppermute(value, axis, [(source, source + steps) for source in range(leading, last)])


def layer_norm(values, gain_row, shift_row):
    center = jnp.mean(values, axis=-1, keepdims=True)
    centered = values - center
    spread = jnp.mean(centered * centered, axis=-1, keepdims=True)
    return centered * lax.rsqrt(spread + epsilon) * gain_row + shift_row


def per_device(
    tokens, ln_gain, ln_bias, w_qkv, b_qkv, w_out, b_out, merge_gain, merge_bias, segments, owners
):
    tok_dev = tokens.shape[0]
    model_width = tokens.shape[1]
    local_width = w_qkv.shape[2]
    local_heads = local_width // HEAD_DIM
    seq_count = lax.axis_size("seq")
    seq_index = lax.axis_index("seq")
    row_start = seq_index * tok_dev
    reach_rows = SPAN * tok_dev
    scale_factor = HEAD_DIM ** (-0.5)
    normed = layer_norm(tokens.astype(jnp.float32), ln_gain, ln_bias).astype(jnp.bfloat16)
    query = (jnp.dot(normed, w_qkv[0], preferred_element_type=jnp.float32) + b_qkv[0]).astype(
        jnp.bfloat16
    )
    key_rows = (jnp.dot(normed, w_qkv[1], preferred_element_type=jnp.float32) + b_qkv[1]).astype(
        jnp.bfloat16
    )
    value_rows = (jnp.dot(normed, w_qkv[2], preferred_element_type=jnp.float32) + b_qkv[2]).astype(
        jnp.bfloat16
    )
    key_value = jnp.concatenate([key_rows, value_rows], axis=1)
    token_segment = jnp.repeat(segments, 4)
    padding = jnp.full((reach_rows,), -1, jnp.int32)
    padded_segment = jnp.concatenate([padding, token_segment, padding])
    query_segment = lax.dynamic_slice_in_dim(token_segment, row_start, tok_dev)
    query_heads = query.reshape(tok_dev, local_heads, HEAD_DIM)

    def segment_window(key_start, length):
        return lax.dynamic_slice_in_dim(padded_segment, key_start + reach_rows, length)

    def block_scores(block, key_segment):
        key_heads = block[:, :local_width].reshape(-1, local_heads, HEAD_DIM)
        value_heads = block[:, local_width:].reshape(-1, local_heads, HEAD_DIM)
        scores = (
            jnp.einsum("qhd,khd->hqk", query_heads, key_heads, preferred_element_type=jnp.float32)
            * scale_factor
        )
        allowed = query_segment[:, None] == key_segment[None, :]
        return (jnp.where(allowed[None], scores, masked_score), value_heads)

    def absorb(state, block, key_segment):
        row_top, totals, summed = state
        scores, value_heads = block_scores(block, key_segment)
        new_top = jnp.maximum(row_top, jnp.max(scores, axis=-1, keepdims=True))
        factor = jnp.exp(row_top - new_top)
        weights = jnp.exp(scores - new_top)
        totals = totals * factor + jnp.sum(weights, axis=-1, keepdims=True)
        summed = summed * factor + jnp.einsum(
            "hqk,khd->hqd",
            weights.astype(jnp.bfloat16),
            value_heads,
            preferred_element_type=jnp.float32,
        )
        return (new_top, totals, summed)

    def absorb_remote(state, block, key_start):
        key_segment = segment_window(key_start, tok_dev)
        return absorb(state, block, key_segment)

    start_state = (
        jnp.full((local_heads, tok_dev, 1), masked_score, jnp.float32),
        jnp.zeros((local_heads, tok_dev, 1), jnp.float32),
        jnp.zeros((local_heads, tok_dev, HEAD_DIM), jnp.float32),
    )
    state = absorb(start_state, key_value, query_segment)
    below = key_value
    above = key_value
    for distance in range(1, SPAN + 1):
        below = from_behind(below, "seq", 1)
        above = from_behind(above, "seq", -1)
        state = absorb_remote(state, below, row_start - distance * tok_dev)
        state = absorb_remote(state, above, row_start + distance * tok_dev)
    row_top, totals, summed = state
    attended = (
        jnp.transpose(summed / totals, (1, 0, 2)).reshape(tok_dev, local_width).astype(jnp.bfloat16)
    )
    tp_index = lax.axis_index("tp")
    quarter = tok_dev // 4
    partial_out = jnp.dot(attended, w_out, preferred_element_type=jnp.float32)
    full_out = lax.psum(partial_out.astype(jnp.bfloat16), "tp").astype(jnp.float32)
    residual = tokens.astype(jnp.float32) + full_out + b_out
    own_rows = lax.dynamic_index_in_dim(
        residual.reshape(quarter, 4, model_width), tp_index, 1, keepdims=False
    )
    merged_rows = layer_norm(own_rows, merge_gain, merge_bias).astype(jnp.bfloat16)
    owner_rows = owners[:, 0]
    capacity = max(2, 2 * quarter // seq_count)
    owner_table = (owner_rows[:, None] == jnp.arange(seq_count, dtype=jnp.int32)[None, :]).astype(
        jnp.int32
    )
    earlier = jnp.cumsum(owner_table, axis=0) - owner_table
    row_slot = jnp.sum(earlier * owner_table, axis=1)
    target_row = owner_rows * capacity + row_slot
    placing = (
        jnp.arange(seq_count * capacity, dtype=jnp.int32)[:, None] == target_row[None, :]
    ).astype(jnp.bfloat16)
    outgoing = jnp.dot(placing, merged_rows, preferred_element_type=jnp.float32).astype(
        jnp.bfloat16
    )
    return lax.all_to_all(outgoing, "seq", split_axis=0, concat_axis=0, tiled=True)


def solution(mesh):
    placed = (
        P("seq", None),
        P(),
        P(),
        P(None, None, "tp"),
        P(None, "tp"),
        P("tp", None),
        P(),
        P(),
        P(),
        P(),
        P("seq", None),
    )
    return jax.shard_map(
        per_device, mesh=mesh, in_specs=placed, out_specs=P("seq", "tp"), check_vma=False
    )
```

profile of v0, /device:TPU:0, one launch (start us, length us, event | category | flops | bytes accessed | tf_op | source)
XLA Modules:
  0.0 155.0 jit_solution(9970447549170431776)
XLA Ops:
  6.5 0.0 all-reduce.2.cloned.1.call-start
  6.6 1.4 convert_reduce_fusion
  8.0 1.4 fusion.11
  9.4 1.7 %fusion.36 = bf16[256,320]{0,1:T(8,128)(2,1)S(1)} fusion(bf16[3,1280,320]{1,2,0:T(8,128)(2,1)} %param.14, f32[320]{0:T(512)S(1)} %get-tuple-element.5, bf16[256,1280]{1,0:T(8,128)(2,1)S(1)} %copy-done.1, f32[1280]{0:T(1024)S(1)} %copy-done.10, f32[1280]{0:T(1024)S(1)} %copy-done.11, f32[256]{0:T(256)S(1)} %add_rsqrt_fusion, f32[256]{0:T(256)S(1)} %broadcast_multiply_fusion), kind=kOutput, calls=%fused_computation.62 | convolution fusion | flops 211845120 | bytes 1651968 | tf_op jit(solution)/shard_map/dot_general | solution.py:43
  11.1 1.7 %fusion.37 = bf16[256,320]{0,1:T(8,128)(2,1)S(1)} fusion(bf16[3,1280,320]{1,2,0:T(8,128)(2,1)} %param.14, f32[320]{0:T(512)S(1)} %get-tuple-element.7, bf16[256,1280]{1,0:T(8,128)(2,1)S(1)} %copy-done.1, f32[1280]{0:T(1024)S(1)} %copy-done.10, f32[1280]{0:T(1024)S(1)} %copy-done.11, f32[256]{0:T(256)S(1)} %add_rsqrt_fusion, f32[256]{0:T(256)S(1)} %broadcast_multiply_fusion), kind=kOutput, calls=%fused_computation.63 | convolution fusion | flops 211845120 | bytes 1651968 | tf_op jit(solution)/shard_map/dot_general | solution.py:46
  12.8 1.3 collective-permute-start.1
  14.1 5.5 %collective-permute-start = (bf16[256,640]{0,1:T(8,128)(2,1)S(1)}, bf16[256,640]{0,1:T(8,128)(2,1)S(1)}, u32[]{:S(2)}, u32[]{:S(2)}) collective-permute-start(bf16[256,640]{0,1:T(8,128)(2,1)S(1)} %pad_maximum_fusion), channel_id=1, source_target_pairs={{0,4},{4,8},{8,12},{12,16},{16,20},{20,24},{24,28},{1,5},{5,9},{9,... | collective-permute-start | bytes 983048 | tf_op jit(solution)/shard_map/ppermute | solution.py:17
  19.7 0.0 copy-start.8
  19.7 0.0 copy-start.9
  19.7 1.7 %fusion.35 = bf16[256,320]{0,1:T(8,128)(2,1)S(1)} fusion(bf16[3,1280,320]{1,2,0:T(8,128)(2,1)} %param.14, f32[320]{0:T(512)S(1)} %get-tuple-element.6, bf16[256,1280]{1,0:T(8,128)(2,1)S(1)} %copy-done.1, f32[1280]{0:T(1024)S(1)} %copy-done.10, f32[1280]{0:T(1024)S(1)} %copy-done.11, f32[256]{0:T(256)S(1)} %add_rsqrt_fusion, f32[256]{0:T(256)S(1)} %broadcast_multiply_fusion), kind=kOutput, calls=%fused_computation.61 | convolution fusion | flops 211845120 | bytes 1651968 | tf_op jit(solution)/shard_map/dot_general | solution.py:40
  21.4 0.1 broadcast_in_dim.133
  21.5 0.2 reshape.637
  21.7 0.1 dynamic_slice.31
  21.8 0.1 fusion.114
  21.9 1.1 broadcast_compare_fusion.6
  23.0 0.1 fusion.85
  23.1 0.1 reduce_window_sum.11
  23.2 0.4 fusion.123
  23.5 1.9 %collective-permute-done.1 = bf16[256,640]{0,1:T(8,128)(2,1)S(1)} collective-permute-done((bf16[256,640]{0,1:T(8,128)(2,1)S(1)}, bf16[256,640]{0,1:T(8,128)(2,1)S(1)}, u32[]{:S(2)}, u32[]{:S(2)}) %collective-permute-start.1) | collective-permute-done | bytes 327712 | tf_op jit(solution)/shard_map/ppermute | solution.py:17
  25.5 1.3 collective-permute-start.3
  26.8 0.4 fusion.121
  27.1 5.5 %collective-permute-done = bf16[256,640]{0,1:T(8,128)(2,1)S(1)} collective-permute-done((bf16[256,640]{0,1:T(8,128)(2,1)S(1)}, bf16[256,640]{0,1:T(8,128)(2,1)S(1)}, u32[]{:S(2)}, u32[]{:S(2)}) %collective-permute-start) | collective-permute-done | bytes 327712 | tf_op jit(solution)/shard_map/ppermute | solution.py:17
  32.6 4.4 %collective-permute-start.2 = (bf16[256,640]{0,1:T(8,128)(2,1)S(1)}, bf16[256,640]{0,1:T(8,128)(2,1)S(1)}, u32[]{:S(2)}, u32[]{:S(2)}) collective-permute-start(bf16[256,640]{0,1:T(8,128)(2,1)S(1)} %collective-permute-done), channel_id=1, source_target_pairs={{0,4},{4,8},{8,12},{12,16},{16,20},{20,24},{24,28},{1,5},{5,9},{9,... | collective-permute-start | bytes 983048 | tf_op jit(solution)/shard_map/ppermute | solution.py:17
  37.0 0.4 fusion.122
  37.4 11.6 %collective-permute-done.2 = bf16[256,640]{0,1:T(8,128)(2,1)S(1)} collective-permute-done((bf16[256,640]{0,1:T(8,128)(2,1)S(1)}, bf16[256,640]{0,1:T(8,128)(2,1)S(1)}, u32[]{:S(2)}, u32[]{:S(2)}) %collective-permute-start.2) | collective-permute-done | bytes 327712 | tf_op jit(solution)/shard_map/ppermute | solution.py:17
  49.0 4.4 %collective-permute-start.4 = (bf16[256,640]{0,1:T(8,128)(2,1)S(1)}, bf16[256,640]{0,1:T(8,128)(2,1)S(1)}, u32[]{:S(2)}, u32[]{:S(2)}) collective-permute-start(bf16[256,640]{0,1:T(8,128)(2,1)S(1)} %collective-permute-done.2), channel_id=1, source_target_pairs={{0,4},{4,8},{8,12},{12,16},{16,20},{20,24},{24,28},{1,5},{5,9},{9,... | collective-permute-start | bytes 983048 | tf_op jit(solution)/shard_map/ppermute | solution.py:17
  53.4 0.4 fusion.120
  53.9 0.4 fusion.119
  54.2 1.3 collective-permute-start.5
  55.6 12.0 %collective-permute-done.4 = bf16[256,640]{0,1:T(8,128)(2,1)S(1)} collective-permute-done((bf16[256,640]{0,1:T(8,128)(2,1)S(1)}, bf16[256,640]{0,1:T(8,128)(2,1)S(1)}, u32[]{:S(2)}, u32[]{:S(2)}) %collective-permute-start.4) | collective-permute-done | bytes 327712 | tf_op jit(solution)/shard_map/ppermute | solution.py:17
  67.6 4.4 %collective-permute-start.6 = (bf16[256,640]{0,1:T(8,128)(2,1)S(1)}, bf16[256,640]{0,1:T(8,128)(2,1)S(1)}, u32[]{:S(2)}, u32[]{:S(2)}) collective-permute-start(bf16[256,640]{0,1:T(8,128)(2,1)S(1)} %collective-permute-done.4), channel_id=1, source_target_pairs={{0,4},{4,8},{8,12},{12,16},{16,20},{20,24},{24,28},{1,5},{5,9},{9,... | collective-permute-start | bytes 983048 | tf_op jit(solution)/shard_map/ppermute | solution.py:17
  72.0 0.4 fusion.118
  72.5 1.3 collective-permute-start.7
  73.8 0.4 fusion.117
  74.1 11.2 %collective-permute-done.6 = bf16[256,640]{0,1:T(8,128)(2,1)S(1)} collective-permute-done((bf16[256,640]{0,1:T(8,128)(2,1)S(1)}, bf16[256,640]{0,1:T(8,128)(2,1)S(1)}, u32[]{:S(2)}, u32[]{:S(2)}) %collective-permute-start.6) | collective-permute-done | bytes 327712 | tf_op jit(solution)/shard_map/ppermute | solution.py:17
  85.3 0.4 fusion.116
  85.8 0.4 fusion.115
  86.2 0.2 fusion.54
  86.3 0.3 fusion.50
  86.7 0.3 fusion.46
  87.0 0.3 fusion.42
  87.3 0.3 fusion.38
  87.6 0.3 fusion.25
  87.9 0.3 fusion.26
  88.2 0.3 fusion.27
  88.5 0.3 fusion.28
  88.9 0.3 fusion.29
  89.2 0.3 fusion.30
  89.5 0.3 fusion.31
  89.8 0.3 fusion.32
  90.1 0.3 fusion.34
  90.4 1.4 convolution_convert_fusion
  91.8 0.0 all-reduce.2.cloned.1.call-update
  91.8 0.2 select_reduce_fusion
  92.0 34.9 %all-reduce.2.cloned.1.call-done = bf16[256,1280]{1,0:T(8,128)(2,1)} async-done(((bf16[256,1280]{1,0:T(8,128)(2,1)}), bf16[256,1280]{1,0:T(8,128)(2,1)}) %all-reduce.2.cloned.1.call-update) | async-done | bytes 655376 | tf_op jit(solution)/shard_map/psum | solution.py:108
  127.0 1.3 fusion.15
  128.2 0.0 copy-start.5
  128.2 0.0 copy-start.6
  128.2 1.4 reshape.657
  129.7 1.9 %fusion.102 = (f32[64]{0:T(128)S(1)}, f32[64,1,1280]{2,1,0:T(1,128)S(1)}) fusion(f32[64,4,1280]{2,1,0:T(4,128)} %reshape.657, s32[]{:T(128)S(6)} %select_n.77), kind=kLoop, calls=%fused_computation.177 | loop fusion | flops 81856 | bytes 655620 | tf_op jit(solution)/shard_map/reduce_sum | solution.py:21
  131.6 0.2 multiply_reduce_fusion
  131.8 0.3 convolution_convert_fusion.1
  132.2 15.3 %all_to_all.12 = bf16[8,16,1280]{2,1,0:T(8,128)(2,1)S(1)} all-to-all(bf16[8,16,1280]{2,1,0:T(8,128)(2,1)S(1)} %bitcast.273), channel_id=1, replica_groups=mesh['seq'=8,'tp'=4] {'seq'}, dimensions={0} | all-to-all | bytes 655360 | tf_op jit(solution)/shard_map/all_to_all | solution.py:128
  147.5 0.7 copy.48
  (43 shorter events, 0.4 us)
Async XLA Ops:
  6.5 83.9 %copy-start = (bf16[320,1280]{1,0:T(8,128)(2,1)S(1)}, bf16[320,1280]{1,0:T(8,128)(2,1)}, u32[]{:S(2)}) copy-start(bf16[320,1280]{1,0:T(8,128)(2,1)} %param.16) | copy-start | bytes 2457604
  6.5 2.9 %copy-start.1 = (bf16[256,1280]{1,0:T(8,128)(2,1)S(1)}, bf16[256,1280]{1,0:T(8,128)(2,1)}, u32[]{:S(2)}) copy-start(bf16[256,1280]{1,0:T(8,128)(2,1)} %param.11) | copy-start | bytes 1966084
  6.5 2.8 %copy-start.7 = (f32[3,320]{1,0:T(4,128)S(1)}, f32[3,320]{1,0:T(4,128)}, u32[]{:S(2)}) copy-start(f32[3,320]{1,0:T(4,128)} %param.15) | copy-start | bytes 11524
  6.5 2.9 %copy-start.10 = (f32[1280]{0:T(1024)S(1)}, f32[1280]{0:T(1024)}, u32[]{:S(2)}) copy-start(f32[1280]{0:T(1024)} %param.13) | copy-start | bytes 15364
  6.5 2.9 %copy-start.11 = (f32[1280]{0:T(1024)S(1)}, f32[1280]{0:T(1024)}, u32[]{:S(2)}) copy-start(f32[1280]{0:T(1024)} %param.12) | copy-start | bytes 15364
  6.5 120.4 %all-reduce.2.cloned.1.call-start = ((), (), s32[]{:S(2)}) async-start(), calls=%async_computation.1 | async-start | bytes 1310720 | tf_op jit(solution)/shard_map/psum | solution.py:108
  12.8 12.6 %collective-permute-start.1 = (bf16[256,640]{0,1:T(8,128)(2,1)S(1)}, bf16[256,640]{0,1:T(8,128)(2,1)S(1)}, u32[]{:S(2)}, u32[]{:S(2)}) collective-permute-start(bf16[256,640]{0,1:T(8,128)(2,1)S(1)} %pad_maximum_fusion), channel_id=1, source_target_pairs={{4,0},{8,4},{12,8},{16,12},{20,16},{24,20},{28,24},{5,1},{9,5},{13... | collective-permute-start | bytes 983048 | tf_op jit(solution)/shard_map/ppermute | solution.py:17
  14.1 18.5 %collective-permute-start = (bf16[256,640]{0,1:T(8,128)(2,1)S(1)}, bf16[256,640]{0,1:T(8,128)(2,1)S(1)}, u32[]{:S(2)}, u32[]{:S(2)}) collective-permute-start(bf16[256,640]{0,1:T(8,128)(2,1)S(1)} %pad_maximum_fusion), channel_id=1, source_target_pairs={{0,4},{4,8},{8,12},{12,16},{16,20},{20,24},{24,28},{1,5},{5,9},{9,... | collective-permute-start | bytes 983048 | tf_op jit(solution)/shard_map/ppermute | solution.py:17
  19.7 1.7 %copy-start.8 = (s32[512]{0:T(512)S(1)}, s32[512]{0:T(512)}, u32[]{:S(2)}) copy-start(s32[512]{0:T(512)} %param.20) | copy-start | bytes 6148
  19.7 3.3 %copy-start.9 = (s32[64,1]{0,1:T(1,128)S(1)}, s32[64,1]{0,1:T(1,128)}, u32[]{:S(2)}) copy-start(s32[64,1]{0,1:T(1,128)} %param.21) | copy-start | bytes 772
  23.1 3.6 %copy-start.3 = (pred[256,256]{0,1:T(8,128)(4,1)S(1)}, pred[256,256]{0,1:T(8,128)(4,1)}, u32[]{:S(2)}) copy-start(pred[256,256]{0,1:T(8,128)(4,1)} %get-tuple-element.55) | copy-start | bytes 196612
  23.5 13.5 %copy-start.2 = (pred[256,256]{0,1:T(8,128)(4,1)S(1)}, pred[256,256]{0,1:T(8,128)(4,1)}, u32[]{:S(2)}) copy-start(pred[256,256]{0,1:T(8,128)(4,1)} %get-tuple-element.62) | copy-start | bytes 196612
  25.5 28.4 %collective-permute-start.3 = (bf16[256,640]{0,1:T(8,128)(2,1)S(1)}, bf16[256,640]{0,1:T(8,128)(2,1)S(1)}, u32[]{:S(2)}, u32[]{:S(2)}) collective-permute-start(bf16[256,640]{0,1:T(8,128)(2,1)S(1)} %collective-permute-done.1), channel_id=1, source_target_pairs={{4,0},{8,4},{12,8},{16,12},{20,16},{24,20},{28,24},{5,1},{9,5},{13... | collective-permute-start | bytes 983048 | tf_op jit(solution)/shard_map/ppermute | solution.py:17
  32.6 16.4 %collective-permute-start.2 = (bf16[256,640]{0,1:T(8,128)(2,1)S(1)}, bf16[256,640]{0,1:T(8,128)(2,1)S(1)}, u32[]{:S(2)}, u32[]{:S(2)}) collective-permute-start(bf16[256,640]{0,1:T(8,128)(2,1)S(1)} %collective-permute-done), channel_id=1, source_target_pairs={{0,4},{4,8},{8,12},{12,16},{16,20},{20,24},{24,28},{1,5},{5,9},{9,... | collective-permute-start | bytes 983048 | tf_op jit(solution)/shard_map/ppermute | solution.py:17
  49.0 18.6 %collective-permute-start.4 = (bf16[256,640]{0,1:T(8,128)(2,1)S(1)}, bf16[256,640]{0,1:T(8,128)(2,1)S(1)}, u32[]{:S(2)}, u32[]{:S(2)}) collective-permute-start(bf16[256,640]{0,1:T(8,128)(2,1)S(1)} %collective-permute-done.2), channel_id=1, source_target_pairs={{0,4},{4,8},{8,12},{12,16},{16,20},{20,24},{24,28},{1,5},{5,9},{9,... | collective-permute-start | bytes 983048 | tf_op jit(solution)/shard_map/ppermute | solution.py:17
  54.2 18.2 %collective-permute-start.5 = (bf16[256,640]{0,1:T(8,128)(2,1)S(1)}, bf16[256,640]{0,1:T(8,128)(2,1)S(1)}, u32[]{:S(2)}, u32[]{:S(2)}) collective-permute-start(bf16[256,640]{0,1:T(8,128)(2,1)S(1)} %collective-permute-done.3), channel_id=1, source_target_pairs={{4,0},{8,4},{12,8},{16,12},{20,16},{24,20},{28,24},{5,1},{9,5},{13... | collective-permute-start | bytes 983048 | tf_op jit(solution)/shard_map/ppermute | solution.py:17
  67.6 17.7 %collective-permute-start.6 = (bf16[256,640]{0,1:T(8,128)(2,1)S(1)}, bf16[256,640]{0,1:T(8,128)(2,1)S(1)}, u32[]{:S(2)}, u32[]{:S(2)}) collective-permute-start(bf16[256,640]{0,1:T(8,128)(2,1)S(1)} %collective-permute-done.4), channel_id=1, source_target_pairs={{0,4},{4,8},{8,12},{12,16},{16,20},{20,24},{24,28},{1,5},{5,9},{9,... | collective-permute-start | bytes 983048 | tf_op jit(solution)/shard_map/ppermute | solution.py:17
  72.5 13.3 %collective-permute-start.7 = (bf16[256,640]{0,1:T(8,128)(2,1)S(1)}, bf16[256,640]{0,1:T(8,128)(2,1)S(1)}, u32[]{:S(2)}, u32[]{:S(2)}) collective-permute-start(bf16[256,640]{0,1:T(8,128)(2,1)S(1)} %collective-permute-done.5), channel_id=1, source_target_pairs={{4,0},{8,4},{12,8},{16,12},{20,16},{24,20},{28,24},{5,1},{9,5},{13... | collective-permute-start | bytes 983048 | tf_op jit(solution)/shard_map/ppermute | solution.py:17
  90.4 36.6 %copy-start.4 = (f32[1280]{0:T(1024)S(1)}, f32[1280]{0:T(1024)}, u32[]{:S(2)}) copy-start(f32[1280]{0:T(1024)} %param.17) | copy-start | bytes 15364
  128.2 3.6 %copy-start.5 = (f32[1280]{0:T(1024)S(1)}, f32[1280]{0:T(1024)}, u32[]{:S(2)}) copy-start(f32[1280]{0:T(1024)} %param.19) | copy-start | bytes 15364
  128.2 3.6 %copy-start.6 = (f32[1280]{0:T(1024)S(1)}, f32[1280]{0:T(1024)}, u32[]{:S(2)}) copy-start(f32[1280]{0:T(1024)} %param.18) | copy-start | bytes 15364
Sparse Core Ops, SparseCore 0:
  91.9 34.9 all-reduce.1
where the time goes:
time: 156 us; the launch traced here: 155 us
  waiting for transfers between devices  77.1 us (49%)
  starting transfers between devices  23.9 us (15%)
  blocking collectives  15.3 us (10%)
  between operations  13.8 us (9%)
  matrix products  12.9 us (8%)
  other arithmetic  9.08 us (6%)
  local copies, waits for them, and re-layouts  2.9 us (2%)
    ppermute x8, waiting for transfers between devices, from_behind(): lax.ppermute(value, axis, [(source, source + steps) for source in range(l...  42.1 us
    psum x1, waiting for transfers between devices, per_device(): lax.psum(partial_out.astype(jnp.bfloat16), 'tp').astype(jnp.float32)  34.9 us
    ppermute x8, starting transfers between devices, from_behind(): lax.ppermute(value, axis, [(source, source + steps) for source in range(l...  23.9 us
    all_to_all x1, blocking collectives, per_device(): lax.all_to_all(outgoing, 'seq', split_axis=0, concat_axis=0, tiled=True)  15.3 us
    dot_general x9, matrix products, block_scores(): jnp.einsum('qhd,khd->hqk', query_heads, key_heads, preferred_element_type...  3.42 us
    reduce_sum x2, other arithmetic, layer_norm(): center = jnp.mean(values, axis=-1, keepdims=True)  3.27 us
  transfers between devices with their start and end apart: 9, of which 6 were waited for; matrix products, arithmetic and copies ran while one was open for 4% of the time, Pallas kernels for 0%

commit v1 on v0

v1 whole, which is shorter than its diff:
```python
import functools

import jax
import jax.numpy as jnp
from jax import lax
from jax.experimental import pallas as pl
from jax.experimental.pallas import tpu as pltpu
from jax.sharding import PartitionSpec as P

HEAD_DIM = 80
MESH = pl.DeviceIdType.MESH

epsilon = 1e-06
masked_score = -1e30


def layer_norm(values, gain_row, shift_row):
    center = jnp.mean(values, axis=-1, keepdims=True)
    centered = values - center
    spread = jnp.mean(centered * centered, axis=-1, keepdims=True)
    return centered * lax.rsqrt(spread + epsilon) * gain_row + shift_row


def iota(shape, dim):
    return lax.broadcasted_iota(jnp.int32, shape, dim)


def kernel(
    n_seq,
    n_tp,
    capacity,
    inside,
    tokens_ref,
    gain_ref,
    bias_ref,
    w_qkv_ref,
    b_qkv_ref,
    w_out_ref,
    b_out_ref,
    merge_gain_ref,
    merge_bias_ref,
    segments_ref,
    owners_ref,
    out_ref,
    kv,
    token_rows,
    normed_ref,
    query_ref,
    top_ref,
    total_ref,
    summed_ref,
    attended_ref,
    terms,
    arrived,
    outgoing,
    kv_send,
    kv_recv,
    tp_send,
    tp_recv,
    route_send,
    route_recv,
):
    tok_dev, model_width = tokens_ref.shape
    local_width = query_ref.shape[1]
    heads = local_width // HEAD_DIM
    quarter = tok_dev // n_tp
    n_pair = n_seq // 2
    me = lax.axis_index("seq")
    t_me = lax.axis_index("tp")
    pair = me // 2
    column = lax.rem(me, 2)
    partner = me + 1 - 2 * column
    has_low = pair > 0
    has_high = pair < n_pair - 1
    has_low2 = pair > 1
    has_high2 = pair < n_pair - 2

    barrier = pltpu.get_barrier_semaphore()
    for k in range(1, n_tp):
        pl.semaphore_signal(
            barrier, inc=1, device_id=(me, lax.rem(t_me + k, n_tp)), device_id_type=MESH
        )
    if inside:
        for k in range(1, n_seq):
            pl.semaphore_signal(
                barrier, inc=1, device_id=(lax.rem(me + k, n_seq), t_me), device_id_type=MESH
            )
    else:
        pl.semaphore_signal(barrier, inc=1, device_id=(partner, t_me), device_id_type=MESH)

        @pl.when(has_low)
        def _():
            pl.semaphore_signal(barrier, inc=1, device_id=(me - 2, t_me), device_id_type=MESH)

        @pl.when(has_high)
        def _():
            pl.semaphore_signal(barrier, inc=1, device_id=(me + 2, t_me), device_id_type=MESH)

    row = iota((tok_dev, tok_dev), 0)
    place = (lax.rem(row, quarter) * n_tp + row // quarter == iota((tok_dev, tok_dev), 1)).astype(
        jnp.bfloat16
    )
    ordered = jnp.dot(place, tokens_ref[...], preferred_element_type=jnp.float32)
    token_rows[...] = ordered.astype(jnp.bfloat16)
    normed_ref[...] = layer_norm(ordered, gain_ref[...], bias_ref[...]).astype(jnp.bfloat16)
    for i in (1, 2):
        kv[0, 2, :, (i - 1) * local_width : i * local_width] = (
            jnp.dot(normed_ref[...], w_qkv_ref[i], preferred_element_type=jnp.float32)
            + b_qkv_ref[i : i + 1, :]
        ).astype(jnp.bfloat16)

    if inside:
        pl.semaphore_wait(barrier, n_tp - 1 + n_seq - 1)
    else:
        pl.semaphore_wait(barrier, n_tp + has_low.astype(jnp.int32) + has_high.astype(jnp.int32))

    def hop(way, src, dst):
        target = (me - 2, me + 2, partner)[way]
        return pltpu.make_async_remote_copy(
            src_ref=kv.at[src[0], src[1]],
            dst_ref=kv.at[dst[0], dst[1]],
            send_sem=kv_send.at[way, src[0], src[1]],
            recv_sem=kv_recv.at[dst[0], dst[1]],
            device_id=(target, t_me),
            device_id_type=MESH,
        )

    low, high, across = 0, 1, 2
    sends = {
        "own": [
            (low, (0, 2), (0, 3), has_low),
            (high, (0, 2), (0, 1), has_high),
            (across, (0, 2), (1, 2), None),
        ],
        "partner": [
            (high, (1, 2), (1, 1), pair == 0),
            (low, (1, 2), (1, 3), pair == n_pair - 1),
        ],
        "low": [
            (high, (0, 1), (0, 0), has_low & has_high),
            (across, (0, 1), (1, 1), has_low & (pair != 1)),
        ],
        "high": [
            (low, (0, 3), (0, 4), has_low & has_high),
            (across, (0, 3), (1, 3), has_high & (pair != n_pair - 2)),
        ],
        "low2": [(across, (0, 0), (1, 0), has_low2 & (column == 1))],
        "high2": [(across, (0, 4), (1, 4), has_high2 & (column == 0))],
    }

    def guarded(condition, action):
        if condition is None:
            action()
        else:
            pl.when(condition)(action)

    def send(name):
        for way, src, dst, condition in sends[name]:
            guarded(condition, lambda: hop(way, src, dst).start())

    def landed(slot, condition):
        def wait():
            hop(across, slot, slot).wait_recv()

        guarded(condition, wait)

    send("own")
    query_ref[...] = (
        jnp.dot(normed_ref[...], w_qkv_ref[0], preferred_element_type=jnp.float32)
        + b_qkv_ref[0:1, :]
    ).astype(jnp.bfloat16)

    def segment_row(block):
        return jnp.concatenate([segments_ref[block]] * n_tp, axis=1)

    scale_factor = HEAD_DIM ** (-0.5)
    own_row = segment_row(me)
    eye = row == iota((tok_dev, tok_dev), 1)
    own_segment = jnp.sum(jnp.where(eye, own_row, 0), axis=1, keepdims=True)

    def absorb(slot, block, first=False):
        allowed = own_segment == segment_row(block)
        for h in range(heads):
            lanes = slice(h * HEAD_DIM, (h + 1) * HEAD_DIM)
            keys = kv[slot[0], slot[1], :, lanes]
            values = kv[
                slot[0], slot[1], :, local_width + h * HEAD_DIM : local_width + (h + 1) * HEAD_DIM
            ]
            scores = (
                lax.dot_general(
                    query_ref[:, lanes],
                    keys,
                    (((1,), (1,)), ((), ())),
                    preferred_element_type=jnp.float32,
                )
                * scale_factor
            )
            scores = jnp.where(allowed, scores, masked_score)
            top = jnp.max(scores, axis=1, keepdims=True)
            if not first:
                old = top_ref[h]
                top = jnp.maximum(old, top)
            weights = jnp.exp(scores - top)
            total = jnp.sum(weights, axis=1, keepdims=True)
            summed = jnp.dot(
                weights.astype(jnp.bfloat16), values, preferred_element_type=jnp.float32
            )
            if not first:
                factor = jnp.exp(old - top)
                total = total_ref[h] * factor + total
                summed = summed_ref[h] * factor + summed
            top_ref[h] = top
            total_ref[h] = total
            summed_ref[h] = summed

    def absorb_if(slot, condition):
        block = 2 * (pair + slot[1] - 2) + (column if slot[0] == 0 else 1 - column)
        guarded(condition, lambda: absorb(slot, block))

    absorb((0, 2), me, first=True)
    landed((1, 2), None)
    send("partner")
    landed((0, 1), has_low)
    send("low")
    landed((0, 3), has_high)
    send("high")
    absorb_if((1, 2), None)
    absorb_if((0, 1), has_low)
    absorb_if((0, 3), has_high)
    landed((0, 0), has_low2)
    send("low2")
    landed((0, 4), has_high2)
    send("high2")
    absorb_if((0, 0), has_low2)
    absorb_if((0, 4), has_high2)
    landed((1, 1), has_low)
    absorb_if((1, 1), has_low)
    landed((1, 3), has_high)
    absorb_if((1, 3), has_high)
    far_low = has_low2 & (column == 0)
    far_high = has_high2 & (column == 1)
    landed((1, 0), far_low)
    absorb_if((1, 0), far_low)
    landed((1, 4), far_high)
    absorb_if((1, 4), far_high)

    for h in range(heads):
        attended_ref[:, h * HEAD_DIM : (h + 1) * HEAD_DIM] = (
            summed_ref[h] / total_ref[h]
        ).astype(jnp.bfloat16)

    def tp_copy(k):
        target = lax.rem(t_me + k, n_tp)
        return pltpu.make_async_remote_copy(
            src_ref=terms.at[target],
            dst_ref=arrived.at[k],
            send_sem=tp_send.at[k],
            recv_sem=tp_recv.at[k],
            device_id=(me, target),
            device_id_type=MESH,
        )

    for k in (2, 3, 1, 0):
        target = lax.rem(t_me + k, n_tp)
        rows = attended_ref[pl.ds(pl.multiple_of(target * quarter, quarter), quarter), :]
        terms[target] = jnp.dot(
            rows, w_out_ref[...], preferred_element_type=jnp.float32
        ).astype(jnp.bfloat16)
        if k:
            tp_copy(k).start()

    lanes = max(n_seq, 128)
    owner = owners_ref[...]
    table = (owner == iota((quarter, lanes), 1)).astype(jnp.float32)
    before = (iota((quarter, quarter), 1) < iota((quarter, quarter), 0)).astype(jnp.bfloat16)
    earlier = jnp.dot(before, table.astype(jnp.bfloat16), preferred_element_type=jnp.float32)
    slot = jnp.sum(earlier * table, axis=1, keepdims=True).astype(jnp.int32)
    goal = owner * capacity + slot
    placing = (goal == iota((quarter, n_seq * capacity), 1)).astype(jnp.bfloat16)

    residual = token_rows[
        pl.ds(pl.multiple_of(t_me * quarter, quarter), quarter), :
    ].astype(jnp.float32)
    head_total = terms[t_me].astype(jnp.float32)
    for k in (1, 3, 2):
        tp_copy(k).wait_recv()
        head_total = head_total + arrived[k].astype(jnp.float32)
    residual = residual + head_total + b_out_ref[...]
    merged = layer_norm(residual, merge_gain_ref[...], merge_bias_ref[...]).astype(jnp.bfloat16)
    placed = lax.dot_general(
        placing, merged, (((0,), (0,)), ((), ())), preferred_element_type=jnp.float32
    ).astype(jnp.bfloat16)

    if inside:
        outgoing[...] = placed.reshape(n_seq, capacity, model_width)

        def route(k):
            target = lax.rem(me + k, n_seq)
            return pltpu.make_async_remote_copy(
                src_ref=outgoing.at[target],
                dst_ref=out_ref.at[me],
                send_sem=route_send.at[k],
                recv_sem=route_recv.at[k],
                device_id=(target, t_me),
                device_id_type=MESH,
            )

        def route_in(k):
            source = lax.rem(me + n_seq - k, n_seq)
            return pltpu.make_async_remote_copy(
                src_ref=outgoing.at[source],
                dst_ref=out_ref.at[source],
                send_sem=route_send.at[k],
                recv_sem=route_recv.at[k],
                device_id=(source, t_me),
                device_id_type=MESH,
            )

        order = sorted(range(1, n_seq), key=lambda k: -abs(n_seq // 2 - k))[::-1]
        for k in order:
            route(k).start()
        out_ref[me] = outgoing[me]
    else:
        out_ref[...] = placed

    for name in sends:
        for way, src, dst, condition in sends[name]:
            guarded(condition, lambda: hop(way, src, dst).wait_send())
    for k in range(1, n_tp):
        tp_copy(k).wait_send()
    if inside:
        for k in order:
            route_in(k).wait_recv()
        for k in order:
            route(k).wait_send()


def per_device(
    tokens, ln_gain, ln_bias, w_qkv, b_qkv, w_out, b_out, merge_gain, merge_bias, segments, owners
):
    tok_dev, model_width = tokens.shape
    local_width = w_qkv.shape[2]
    heads = local_width // HEAD_DIM
    n_seq = lax.axis_size("seq")
    n_tp = lax.axis_size("tp")
    quarter = tok_dev // n_tp
    capacity = max(2, 2 * quarter // n_seq)
    inside = capacity % 16 == 0
    out_shape = (n_seq, capacity, model_width) if inside else (n_seq * capacity, model_width)
    vmem = pl.BlockSpec(memory_space=pltpu.VMEM)
    routed = pl.pallas_call(
        functools.partial(kernel, n_seq, n_tp, capacity, inside),
        out_shape=jax.ShapeDtypeStruct(out_shape, jnp.bfloat16),
        in_specs=[vmem] * 11,
        out_specs=vmem,
        scratch_shapes=[
            pltpu.VMEM((2, 5, tok_dev, 2 * local_width), jnp.bfloat16),
            pltpu.VMEM((tok_dev, model_width), jnp.bfloat16),
            pltpu.VMEM((tok_dev, model_width), jnp.bfloat16),
            pltpu.VMEM((tok_dev, local_width), jnp.bfloat16),
            pltpu.VMEM((heads, tok_dev, 1), jnp.float32),
            pltpu.VMEM((heads, tok_dev, 1), jnp.float32),
            pltpu.VMEM((heads, tok_dev, HEAD_DIM), jnp.float32),
            pltpu.VMEM((tok_dev, local_width), jnp.bfloat16),
            pltpu.VMEM((n_tp, quarter, model_width), jnp.bfloat16),
            pltpu.VMEM((n_tp, quarter, model_width), jnp.bfloat16),
            pltpu.VMEM((n_seq, max(capacity, 16), model_width) if inside else (1, 16, 128), jnp.bfloat16),
            pltpu.SemaphoreType.DMA((3, 2, 5)),
            pltpu.SemaphoreType.DMA((2, 5)),
            pltpu.SemaphoreType.DMA((n_tp,)),
            pltpu.SemaphoreType.DMA((n_tp,)),
            pltpu.SemaphoreType.DMA((n_seq,)),
            pltpu.SemaphoreType.DMA((n_seq,)),
        ],
        compiler_params=pltpu.CompilerParams(
            collective_id=0, has_side_effects=True, vmem_limit_bytes=48 * 1024 * 1024
        ),
        cost_estimate=pl.CostEstimate(
            flops=2 * 10**9, bytes_accessed=5 * 10**6, transcendentals=3 * 10**6
        ),
    )(
        tokens,
        ln_gain[None, :],
        ln_bias[None, :],
        w_qkv,
        b_qkv,
        w_out,
        b_out[None, :],
        merge_gain[None, :],
        merge_bias[None, :],
        segments.reshape(n_seq, 1, quarter),
        owners,
    )
    if inside:
        return routed.reshape(n_seq * capacity, model_width)
    return lax.all_to_all(routed, "seq", split_axis=0, concat_axis=0, tiled=True)


def solution(mesh):
    placed = (
        P("seq", None),
        P(),
        P(),
        P(None, None, "tp"),
        P(None, "tp"),
        P("tp", None),
        P(),
        P(),
        P(),
        P(),
        P("seq", None),
    )
    return jax.shard_map(
        per_device, mesh=mesh, in_specs=placed, out_specs=P("seq", "tp"), check_vma=False
    )
```

time: 156 us -> 59.5 us (0.38)
  the two profiles are of different devices: /device:TPU:0 before, /device:TPU:17 now
where the time goes in v1:
time: 59.5 us; the launch traced here: 58.9 us
  Pallas kernels  46.8 us (79%)
  local copies, waits for them, and re-layouts  12.1 us (20%)
    pallas_call x1, Pallas kernels, per_device(): pl.pallas_call(functools.partial(kernel, n_seq, n_tp, capacity, inside),...  46.8 us
    unnamed x9, local copies, waits for them, and re-layouts  7.78 us

profile of v1, /device:TPU:17, one launch (start us, length us, event | category | flops | bytes accessed | tf_op | source)
XLA Modules:
  0.0 58.9 jit_solution(2670630324307718475)
XLA Ops:
  0.0 0.0 copy-start.2
  0.0 0.8 %reshape.6.segments_ref = s32[8,1,64]{2,1,0:T(1,128)S(1)} reshape(s32[512]{0:T(512)} %param.20) | data formatting | bytes 4096 | tf_op jit(solution)/shard_map/reshape | solution.py:391
  0.8 0.7 %broadcast_in_dim.15.gain_ref = f32[1,1280]{1,0:T(1,128)S(1)} reshape(f32[1280]{0:T(1024)} %param.12) | data formatting | bytes 10240 | tf_op jit(solution)/shard_map/broadcast_in_dim | solution.py:383
  1.5 0.7 %broadcast_in_dim.16.bias_ref = f32[1,1280]{1,0:T(1,128)S(1)} reshape(f32[1280]{0:T(1024)} %param.13) | data formatting | bytes 10240 | tf_op jit(solution)/shard_map/broadcast_in_dim | solution.py:384
  2.2 0.7 %broadcast_in_dim.17.b_out_ref = f32[1,1280]{1,0:T(1,128)S(1)} reshape(f32[1280]{0:T(1024)} %param.17) | data formatting | bytes 10240 | tf_op jit(solution)/shard_map/broadcast_in_dim | solution.py:388
  2.9 0.7 %broadcast_in_dim.18.merge_gain_ref = f32[1,1280]{1,0:T(1,128)S(1)} reshape(f32[1280]{0:T(1024)} %param.18) | data formatting | bytes 10240 | tf_op jit(solution)/shard_map/broadcast_in_dim | solution.py:389
  3.6 0.7 %broadcast_in_dim.19.merge_bias_ref = f32[1,1280]{1,0:T(1,128)S(1)} reshape(f32[1280]{0:T(1024)} %param.19) | data formatting | bytes 10240 | tf_op jit(solution)/shard_map/broadcast_in_dim | solution.py:390
  4.3 0.7 %copy.13.owners_ref = s32[64,1]{1,0:T(8,128)S(1)} copy(s32[64,1]{0,1:T(1,128)} %param.21) | data formatting | bytes 512 | tf_op args[10]
  5.0 4.1 %copy.12.w_qkv_ref = bf16[3,1280,320]{2,1,0:T(8,128)(2,1)S(1)} copy(bf16[3,1280,320]{1,2,0:T(8,128)(2,1)} %param.14) | data formatting | bytes 4915200 | tf_op args[3]
  9.1 0.0 copy-done.2
  9.1 0.0 copy-start
  9.1 1.1 %copy-done = bf16[320,1280]{1,0:T(8,128)(2,1)S(1)} copy-done((bf16[320,1280]{1,0:T(8,128)(2,1)S(1)}, bf16[320,1280]{1,0:T(8,128)(2,1)}, u32[]{:S(2)}) %copy-start) | copy-done | bytes 819224
  10.3 0.0 copy-start.1
  10.3 1.1 %copy-done.1 = bf16[256,1280]{1,0:T(8,128)(2,1)S(1)} copy-done((bf16[256,1280]{1,0:T(8,128)(2,1)S(1)}, bf16[256,1280]{1,0:T(8,128)(2,1)}, u32[]{:S(2)}) %copy-start.1) | copy-done | bytes 655384
  11.4 46.8 %shard_map.109 = bf16[8,16,1280]{2,1,0:T(8,128)(2,1)S(1)} custom-call(bf16[256,1280]{1,0:T(8,128)(2,1)S(1)} %copy-done.1, f32[1,1280]{1,0:T(1,128)S(1)} %broadcast_in_dim.15.gain_ref, f32[1,1280]{1,0:T(1,128)S(1)} %broadcast_in_dim.16.bias_ref, bf16[3,1280,320]{2,1,0:T(8,128)(2,1)S(1)} %copy.12.w_qkv_ref, f32[3,320]{1,0:T(4,128)S(1)} %copy-done.2, ...), custom_call_target="tpu_custom_call" | custom-call | flops 2000000000 | bytes 5000000 | tf_op jit(solution)/shard_map/pallas_call | solution.py:351
  58.2 0.7 %copy.15 = bf16[128,1280]{1,0:T(8,128)(2,1)} copy(bf16[128,1280]{1,0:T(8,128)(2,1)S(1)} %bitcast.1) | data formatting | bytes 655360
Async XLA Ops:
  0.0 9.1 %copy-start.2 = (f32[3,320]{1,0:T(4,128)S(1)}, f32[3,320]{1,0:T(4,128)}, u32[]{:S(2)}) copy-start(f32[3,320]{1,0:T(4,128)} %b_qkv_ref.1) | copy-start | bytes 11524
  9.1 1.1 %copy-start = (bf16[320,1280]{1,0:T(8,128)(2,1)S(1)}, bf16[320,1280]{1,0:T(8,128)(2,1)}, u32[]{:S(2)}) copy-start(bf16[320,1280]{1,0:T(8,128)(2,1)} %w_out_ref.1) | copy-start | bytes 2457604
  10.3 1.1 %copy-start.1 = (bf16[256,1280]{1,0:T(8,128)(2,1)S(1)}, bf16[256,1280]{1,0:T(8,128)(2,1)}, u32[]{:S(2)}) copy-start(bf16[256,1280]{1,0:T(8,128)(2,1)} %tokens_ref.1) | copy-start | bytes 1966084

commit v2 on v1

v2 whole, which is shorter than its diff:
```python
import functools
import math

import jax
import jax.numpy as jnp
from jax import lax
from jax.experimental import pallas as pl
from jax.experimental.pallas import tpu as pltpu
from jax.sharding import PartitionSpec as P

HEAD_DIM = 80
MESH = pl.DeviceIdType.MESH

epsilon = 1e-06
masked_score = -1e30


def layer_norm(values, gain_row, shift_row):
    center = jnp.mean(values, axis=-1, keepdims=True)
    centered = values - center
    spread = jnp.mean(centered * centered, axis=-1, keepdims=True)
    return centered * lax.rsqrt(spread + epsilon) * gain_row + shift_row


def row_of(ref):
    return ref[...].reshape(1, ref.shape[0])


def iota(shape, dim):
    return lax.broadcasted_iota(jnp.int32, shape, dim)


def kernel(
    n_seq,
    n_tp,
    capacity,
    inside,
    tokens_hbm,
    gain_ref,
    bias_ref,
    w_qkv_hbm,
    b_qkv_ref,
    w_out_hbm,
    b_out_ref,
    merge_gain_ref,
    merge_bias_ref,
    segments_ref,
    owners_ref,
    out_ref,
    tokens_ref,
    w_qkv_ref,
    w_out_ref,
    segment_rows,
    kv,
    token_rows,
    normed_ref,
    query_ref,
    top_ref,
    total_ref,
    summed_ref,
    attended_ref,
    terms,
    arrived,
    pair_sum,
    outgoing,
    load_sem,
    kv_send,
    kv_recv,
    tp_send,
    tp_recv,
    route_send,
    route_recv,
):
    tok_dev, model_width = tokens_ref.shape
    local_width = query_ref.shape[1]
    heads = local_width // HEAD_DIM
    quarter = tok_dev // n_tp
    n_pair = n_seq // 2
    me = lax.axis_index("seq")
    t_me = lax.axis_index("tp")
    pair = me // 2
    column = lax.rem(me, 2)
    partner = me + 1 - 2 * column
    has_low = pair > 0
    has_high = pair < n_pair - 1
    has_low2 = pair > 1
    has_high2 = pair < n_pair - 2

    loads = [
        pltpu.make_async_copy(tokens_hbm, tokens_ref, load_sem.at[0]),
        pltpu.make_async_copy(w_qkv_hbm.at[1], w_qkv_ref.at[1], load_sem.at[1]),
        pltpu.make_async_copy(w_qkv_hbm.at[2], w_qkv_ref.at[2], load_sem.at[2]),
        pltpu.make_async_copy(w_qkv_hbm.at[0], w_qkv_ref.at[0], load_sem.at[3]),
        pltpu.make_async_copy(w_out_hbm, w_out_ref, load_sem.at[4]),
    ]
    for load in loads:
        load.start()

    barrier = pltpu.get_barrier_semaphore()
    for k in range(1, n_tp):
        pl.semaphore_signal(
            barrier, inc=1, device_id=(me, lax.rem(t_me + k, n_tp)), device_id_type=MESH
        )
    if inside:
        for k in range(1, n_seq):
            pl.semaphore_signal(
                barrier, inc=1, device_id=(lax.rem(me + k, n_seq), t_me), device_id_type=MESH
            )
    else:
        pl.semaphore_signal(barrier, inc=1, device_id=(partner, t_me), device_id_type=MESH)

        @pl.when(has_low)
        def _():
            pl.semaphore_signal(barrier, inc=1, device_id=(me - 2, t_me), device_id_type=MESH)

        @pl.when(has_high)
        def _():
            pl.semaphore_signal(barrier, inc=1, device_id=(me + 2, t_me), device_id_type=MESH)

    row = iota((tok_dev, tok_dev), 0)
    place = (lax.rem(row, quarter) * n_tp + row // quarter == iota((tok_dev, tok_dev), 1)).astype(
        jnp.bfloat16
    )
    loads[0].wait()
    ordered = jnp.dot(place, tokens_ref[...], preferred_element_type=jnp.float32)
    token_rows[...] = ordered.astype(jnp.bfloat16)
    normed_ref[...] = layer_norm(ordered, row_of(gain_ref), row_of(bias_ref)).astype(jnp.bfloat16)

    def project(i):
        return (
            lax.dot_general(
                normed_ref[...],
                w_qkv_ref[i],
                (((1,), (1,)), ((), ())),
                preferred_element_type=jnp.float32,
            )
            + b_qkv_ref[i : i + 1, :]
        ).astype(jnp.bfloat16)

    loads[1].wait()
    kv[0, 2, 0] = project(1)

    if inside:
        pl.semaphore_wait(barrier, n_tp - 1 + n_seq - 1)
    else:
        pl.semaphore_wait(barrier, n_tp + has_low.astype(jnp.int32) + has_high.astype(jnp.int32))

    def hop(way, src, dst, half):
        target = (me - 2, me + 2, partner)[way]
        return pltpu.make_async_remote_copy(
            src_ref=kv.at[src[0], src[1], half],
            dst_ref=kv.at[dst[0], dst[1], half],
            send_sem=kv_send.at[way, src[0], src[1], half],
            recv_sem=kv_recv.at[dst[0], dst[1], half],
            device_id=(target, t_me),
            device_id_type=MESH,
        )

    low, high, across = 0, 1, 2
    at_first = pair == 0
    at_last = pair == n_pair - 1
    sends = {
        "own": [
            (low, (0, 2), (0, 3), has_low, has_low),
            (high, (0, 2), (0, 1), has_high, has_high),
            (across, (0, 2), (1, 2), None, None),
        ],
        "partner": [
            (high, (1, 2), (1, 1), at_first, at_first | (has_high & (column == 0))),
            (low, (1, 2), (1, 3), at_last, at_last | (has_low & (column == 1))),
        ],
        "low": [
            (high, (0, 1), (0, 0), has_low & has_high, has_low & has_high),
            (
                across,
                (0, 1),
                (1, 1),
                has_low & (pair != 1),
                has_low & (pair != 1) & (column == 0),
            ),
        ],
        "high": [
            (low, (0, 3), (0, 4), has_low & has_high, has_low & has_high),
            (
                across,
                (0, 3),
                (1, 3),
                has_high & (pair != n_pair - 2),
                has_high & (pair != n_pair - 2) & (column == 1),
            ),
        ],
        "low2": [
            (across, (0, 0), (1, 0), has_low2 & (column == 1), has_low2 & (column == 1))
        ],
        "high2": [
            (across, (0, 4), (1, 4), has_high2 & (column == 0), has_high2 & (column == 0))
        ],
    }

    def guarded(condition, action):
        if condition is None:
            action()
        else:
            pl.when(condition)(action)

    def send(name, half):
        for way, src, dst, *conditions in sends[name]:
            guarded(conditions[half], lambda: hop(way, src, dst, half).start())

    def landed(slot, half, condition):
        guarded(condition, lambda: hop(across, slot, slot, half).wait_recv())

    send("own", 0)
    loads[2].wait()
    kv[0, 2, 1] = project(2)
    send("own", 1)
    loads[3].wait()
    query_ref[...] = project(0)

    segments = row_of(segments_ref)
    for block in range(n_seq):
        segment_rows[block] = jnp.concatenate(
            [segments[:, block * quarter : (block + 1) * quarter]] * n_tp, axis=1
        )

    def segment_row(block):
        return segment_rows[block]

    exponent_scale = HEAD_DIM ** (-0.5) * math.log2(math.e)
    own_row = segment_row(me)
    eye = row == iota((tok_dev, tok_dev), 1)
    own_segment = jnp.sum(jnp.where(eye, own_row, 0), axis=1, keepdims=True)

    def absorb(slot, block, first=False):
        allowed = own_segment == segment_row(block)
        for h in range(heads):
            lanes = slice(h * HEAD_DIM, (h + 1) * HEAD_DIM)
            keys = kv[slot[0], slot[1], 0, :, lanes]
            values = kv[slot[0], slot[1], 1, :, lanes]
            scores = lax.dot_general(
                query_ref[:, lanes],
                keys,
                (((1,), (1,)), ((), ())),
                preferred_element_type=jnp.float32,
            )
            scores = jnp.where(allowed, scores, masked_score)
            top = jnp.max(scores, axis=1, keepdims=True)
            if not first:
                old = top_ref[h]
                top = jnp.maximum(old, top)
            weights = jnp.exp2((scores - top) * exponent_scale)
            total = jnp.sum(weights, axis=1, keepdims=True)
            summed = jnp.dot(
                weights.astype(jnp.bfloat16), values, preferred_element_type=jnp.float32
            )
            if not first:
                factor = jnp.exp2((old - top) * exponent_scale)
                total = total_ref[h] * factor + total
                summed = summed_ref[h] * factor + summed
            top_ref[h] = top
            total_ref[h] = total
            summed_ref[h] = summed

    def absorb_if(slot, condition):
        block = 2 * (pair + slot[1] - 2) + (column if slot[0] == 0 else 1 - column)
        guarded(condition, lambda: absorb(slot, block))

    absorb((0, 2), me, first=True)
    for half in (0, 1):
        landed((0, 1), half, has_low)
        send("low", half)
        landed((0, 3), half, has_high)
        send("high", half)
        landed((1, 2), half, None)
        send("partner", half)
    absorb_if((1, 2), None)
    absorb_if((0, 1), has_low)
    absorb_if((0, 3), has_high)
    for half in (0, 1):
        landed((0, 0), half, has_low2)
        send("low2", half)
        landed((0, 4), half, has_high2)
        send("high2", half)
    absorb_if((0, 0), has_low2)
    absorb_if((0, 4), has_high2)
    far_low = has_low2 & (column == 0)
    far_high = has_high2 & (column == 1)
    for slot, condition in (
        ((1, 1), has_low),
        ((1, 3), has_high),
        ((1, 0), far_low),
        ((1, 4), far_high),
    ):
        for half in (0, 1):
            landed(slot, half, condition)
        absorb_if(slot, condition)

    for h in range(heads):
        attended_ref[:, h * HEAD_DIM : (h + 1) * HEAD_DIM] = (
            summed_ref[h] / total_ref[h]
        ).astype(jnp.bfloat16)

    opposite = lax.rem(t_me + n_tp // 2, n_tp)
    sibling = t_me + 1 - 2 * lax.rem(t_me, 2)
    diagonal = lax.rem(sibling + n_tp // 2, n_tp)

    def tp_copy(k):
        return pltpu.make_async_remote_copy(
            src_ref=(terms.at[diagonal], terms.at[sibling], pair_sum)[k],
            dst_ref=arrived.at[k],
            send_sem=tp_send.at[k],
            recv_sem=tp_recv.at[k],
            device_id=(me, (sibling, sibling, opposite)[k]),
            device_id_type=MESH,
        )

    loads[4].wait()

    def term(target):
        rows = attended_ref[pl.ds(pl.multiple_of(target * quarter, quarter), quarter), :]
        terms[target] = jnp.dot(
            rows, w_out_ref[...], preferred_element_type=jnp.float32
        ).astype(jnp.bfloat16)

    term(diagonal)
    tp_copy(0).start()
    term(opposite)
    tp_copy(0).wait_recv()
    pair_sum[...] = (
        terms[opposite].astype(jnp.float32) + arrived[0].astype(jnp.float32)
    ).astype(jnp.bfloat16)
    tp_copy(2).start()
    term(sibling)
    tp_copy(1).start()
    term(t_me)

    lanes = max(n_seq, 128)
    own_lane = iota((quarter, quarter), 0) == iota((quarter, quarter), 1)
    owner = jnp.sum(jnp.where(own_lane, owners_ref[...], 0), axis=1, keepdims=True)
    table = (owner == iota((quarter, lanes), 1)).astype(jnp.float32)
    before = (iota((quarter, quarter), 1) < iota((quarter, quarter), 0)).astype(jnp.bfloat16)
    earlier = jnp.dot(before, table.astype(jnp.bfloat16), preferred_element_type=jnp.float32)
    slot = jnp.sum(earlier * table, axis=1, keepdims=True).astype(jnp.int32)
    goal = owner * capacity + slot
    placing = (goal == iota((quarter, n_seq * capacity), 1)).astype(jnp.bfloat16)

    residual = token_rows[
        pl.ds(pl.multiple_of(t_me * quarter, quarter), quarter), :
    ].astype(jnp.float32)
    head_total = terms[t_me].astype(jnp.float32)
    for k in (1, 2):
        tp_copy(k).wait_recv()
        head_total = head_total + arrived[k].astype(jnp.float32)
    residual = residual + head_total + row_of(b_out_ref)
    merged = layer_norm(residual, row_of(merge_gain_ref), row_of(merge_bias_ref)).astype(jnp.bfloat16)
    placed = lax.dot_general(
        placing, merged, (((0,), (0,)), ((), ())), preferred_element_type=jnp.float32
    ).astype(jnp.bfloat16)

    if inside:
        outgoing[...] = placed.reshape(n_seq, capacity, model_width)

        def route(k):
            target = lax.rem(me + k, n_seq)
            return pltpu.make_async_remote_copy(
                src_ref=outgoing.at[target],
                dst_ref=out_ref.at[me],
                send_sem=route_send.at[k],
                recv_sem=route_recv.at[k],
                device_id=(target, t_me),
                device_id_type=MESH,
            )

        def route_in(k):
            source = lax.rem(me + n_seq - k, n_seq)
            return pltpu.make_async_remote_copy(
                src_ref=outgoing.at[source],
                dst_ref=out_ref.at[source],
                send_sem=route_send.at[k],
                recv_sem=route_recv.at[k],
                device_id=(source, t_me),
                device_id_type=MESH,
            )

        order = sorted(range(1, n_seq), key=lambda k: -abs(n_seq // 2 - k))[::-1]
        for k in order:
            route(k).start()
        out_ref[me] = outgoing[me]
    else:
        out_ref[...] = placed

    for name in sends:
        for way, src, dst, *conditions in sends[name]:
            for half in (0, 1):
                guarded(conditions[half], lambda: hop(way, src, dst, half).wait_send())
    for k in range(3):
        tp_copy(k).wait_send()
    if inside:
        for k in order:
            route_in(k).wait_recv()
        for k in order:
            route(k).wait_send()


def per_device(
    tokens, ln_gain, ln_bias, w_qkv, b_qkv, w_out, b_out, merge_gain, merge_bias, segments, owners
):
    tok_dev, model_width = tokens.shape
    local_width = w_qkv.shape[2]
    heads = local_width // HEAD_DIM
    n_seq = lax.axis_size("seq")
    n_tp = lax.axis_size("tp")
    quarter = tok_dev // n_tp
    capacity = max(2, 2 * quarter // n_seq)
    inside = capacity % 16 == 0
    out_shape = (n_seq, capacity, model_width) if inside else (n_seq * capacity, model_width)
    vmem = pl.BlockSpec(memory_space=pltpu.VMEM)
    hbm = pl.BlockSpec(memory_space=pltpu.HBM)
    routed = pl.pallas_call(
        functools.partial(kernel, n_seq, n_tp, capacity, inside),
        out_shape=jax.ShapeDtypeStruct(out_shape, jnp.bfloat16),
        in_specs=[hbm, vmem, vmem, hbm, vmem, hbm] + [vmem] * 5,
        out_specs=vmem,
        scratch_shapes=[
            pltpu.VMEM((tok_dev, model_width), jnp.bfloat16),
            pltpu.VMEM((3, local_width, model_width), jnp.bfloat16),
            pltpu.VMEM((local_width, model_width), jnp.bfloat16),
            pltpu.VMEM((n_seq, 1, tok_dev), jnp.int32),
            pltpu.VMEM((2, 5, 2, tok_dev, local_width), jnp.bfloat16),
            pltpu.VMEM((tok_dev, model_width), jnp.bfloat16),
            pltpu.VMEM((tok_dev, model_width), jnp.bfloat16),
            pltpu.VMEM((tok_dev, local_width), jnp.bfloat16),
            pltpu.VMEM((heads, tok_dev, 1), jnp.float32),
            pltpu.VMEM((heads, tok_dev, 1), jnp.float32),
            pltpu.VMEM((heads, tok_dev, HEAD_DIM), jnp.float32),
            pltpu.VMEM((tok_dev, local_width), jnp.bfloat16),
            pltpu.VMEM((n_tp, quarter, model_width), jnp.bfloat16),
            pltpu.VMEM((3, quarter, model_width), jnp.bfloat16),
            pltpu.VMEM((quarter, model_width), jnp.bfloat16),
            pltpu.VMEM((n_seq, max(capacity, 16), model_width) if inside else (1, 16, 128), jnp.bfloat16),
            pltpu.SemaphoreType.DMA((5,)),
            pltpu.SemaphoreType.DMA((3, 2, 5, 2)),
            pltpu.SemaphoreType.DMA((2, 5, 2)),
            pltpu.SemaphoreType.DMA((3,)),
            pltpu.SemaphoreType.DMA((3,)),
            pltpu.SemaphoreType.DMA((n_seq,)),
            pltpu.SemaphoreType.DMA((n_seq,)),
        ],
        compiler_params=pltpu.CompilerParams(
            collective_id=0, has_side_effects=True, vmem_limit_bytes=60 * 1024 * 1024
        ),
        cost_estimate=pl.CostEstimate(
            flops=2 * 10**9, bytes_accessed=5 * 10**6, transcendentals=3 * 10**6
        ),
    )(
        tokens,
        ln_gain,
        ln_bias,
        jnp.swapaxes(w_qkv, 1, 2),
        b_qkv,
        w_out,
        b_out,
        merge_gain,
        merge_bias,
        segments,
        owners.T,
    )
    if inside:
        return routed.reshape(n_seq * capacity, model_width)
    return lax.all_to_all(routed, "seq", split_axis=0, concat_axis=0, tiled=True)


def solution(mesh):
    placed = (
        P("seq", None),
        P(),
        P(),
        P(None, None, "tp"),
        P(None, "tp"),
        P("tp", None),
        P(),
        P(),
        P(),
        P(),
        P("seq", None),
    )
    return jax.shard_map(
        per_device, mesh=mesh, in_specs=placed, out_specs=P("seq", "tp"), check_vma=False
    )
```

time: 59.5 us -> 53.2 us (0.89)
  the two profiles are of different devices: /device:TPU:17 before, /device:TPU:0 now
where the time goes in v2:
time: 53.2 us; the launch traced here: 53 us
  Pallas kernels  51.3 us (96%)
  local copies, waits for them, and re-layouts  1.72 us (3%)
    pallas_call x1, Pallas kernels, per_device(): pl.pallas_call(functools.partial(kernel, n_seq, n_tp, capacity, inside),...  51.3 us
    unnamed x1, local copies, waits for them, and re-layouts  1.72 us

profile of v2, /device:TPU:0, one launch (start us, length us, event | category | flops | bytes accessed | tf_op | source)
XLA Modules:
  0.0 53.0 jit_solution(10567458653031418952)
XLA Ops:
  0.0 51.3 %shard_map.109 = bf16[8,16,1280]{2,1,0:T(8,128)(2,1)} custom-call(bf16[256,1280]{1,0:T(8,128)(2,1)} %tokens_hbm.1, f32[1280]{0:T(1024)} %gain_ref.1, f32[1280]{0:T(1024)} %bias_ref.1, bf16[3,320,1280]{2,1,0:T(8,128)(2,1)} %bitcast.4, f32[3,320]{1,0:T(4,128)} %b_qkv_ref.1, bf16[320,1280]{1,0:T(8,128)(2,1)} %w_out_hbm.1, f32[1280]{0:T(1024)} %b_out_ref.1, ...), custom_call_target="tpu_custom_call" | custom-call | flops 2000000000 | bytes 5000000 | tf_op jit(solution)/shard_map/pallas_call | solution.py:419
  51.3 1.7 %copy.13 = bf16[128,1280]{1,0:T(8,128)(2,1)} copy(bf16[128,1280]{1,0:T(8,128)(2,1)} %bitcast.3) | data formatting | bytes 655360

commit v3 on v2

--- a/solution.py
+++ b/solution.py
@@ -231,27 +231,43 @@
     eye = row == iota((tok_dev, tok_dev), 1)
     own_segment = jnp.sum(jnp.where(eye, own_row, 0), axis=1, keepdims=True)
 
-    def absorb(slot, block, first=False):
-        allowed = own_segment == segment_row(block)
+    def block_of(slot):
+        return 2 * (pair + slot[1] - 2) + (column if slot[0] == 0 else 1 - column)
+
+    def absorb(slots, first=False):
+        allowed = [own_segment == segment_row(block_of(slot)) for slot in slots]
         for h in range(heads):
             lanes = slice(h * HEAD_DIM, (h + 1) * HEAD_DIM)
-            keys = kv[slot[0], slot[1], 0, :, lanes]
-            values = kv[slot[0], slot[1], 1, :, lanes]
-            scores = lax.dot_general(
-                query_ref[:, lanes],
-                keys,
-                (((1,), (1,)), ((), ())),
-                preferred_element_type=jnp.float32,
-            )
-            scores = jnp.where(allowed, scores, masked_score)
-            top = jnp.max(scores, axis=1, keepdims=True)
+            query = query_ref[:, lanes]
+            scores = [
+                jnp.where(
+                    mask,
+                    lax.dot_general(
+                        query,
+                        kv[slot[0], slot[1], 0, :, lanes],
+                        (((1,), (1,)), ((), ())),
+                        preferred_element_type=jnp.float32,
+                    ),
+                    masked_score,
+                )
+                for slot, mask in zip(slots, allowed)
+            ]
+            top = jnp.max(functools.reduce(jnp.maximum, scores), axis=1, keepdims=True)
             if not first:
                 old = top_ref[h]
                 top = jnp.maximum(old, top)
-            weights = jnp.exp2((scores - top) * exponent_scale)
-            total = jnp.sum(weights, axis=1, keepdims=True)
-            summed = jnp.dot(
-                weights.astype(jnp.bfloat16), values, preferred_element_type=jnp.float32
+            weights = [jnp.exp2((part - top) * exponent_scale) for part in scores]
+            total = jnp.sum(functools.reduce(jnp.add, weights), axis=1, keepdims=True)
+            summed = functools.reduce(
+                jnp.add,
+                [
+                    jnp.dot(
+                        part.astype(jnp.bfloat16),
+                        kv[slot[0], slot[1], 1, :, lanes],
+                        preferred_element_type=jnp.float32,
+                    )
+                    for slot, part in zip(slots, weights)
+                ],
             )
             if not first:
                 factor = jnp.exp2((old - top) * exponent_scale)
@@ -262,10 +278,14 @@
             summed_ref[h] = summed
 
     def absorb_if(slot, condition):
-        block = 2 * (pair + slot[1] - 2) + (column if slot[0] == 0 else 1 - column)
-        guarded(condition, lambda: absorb(slot, block))
-
-    absorb((0, 2), me, first=True)
+        guarded(condition, lambda: absorb([slot]))
+
+    def absorb_both(low_slot, high_slot):
+        guarded(has_low & has_high, lambda: absorb([low_slot, high_slot]))
+        guarded(has_low & jnp.logical_not(has_high), lambda: absorb([low_slot]))
+        guarded(has_high & jnp.logical_not(has_low), lambda: absorb([high_slot]))
+
+    absorb([(0, 2)], first=True)
     for half in (0, 1):
         landed((0, 1), half, has_low)
         send("low", half)
@@ -274,23 +294,22 @@
         landed((1, 2), half, None)
         send("partner", half)
     absorb_if((1, 2), None)
-    absorb_if((0, 1), has_low)
-    absorb_if((0, 3), has_high)
     for half in (0, 1):
         landed((0, 0), half, has_low2)
         send("low2", half)
         landed((0, 4), half, has_high2)
         send("high2", half)
+        if half == 0:
+            absorb_both((0, 1), (0, 3))
     absorb_if((0, 0), has_low2)
     absorb_if((0, 4), has_high2)
+    for half in (0, 1):
+        landed((1, 1), half, has_low)
+        landed((1, 3), half, has_high)
+    absorb_both((1, 1), (1, 3))
     far_low = has_low2 & (column == 0)
     far_high = has_high2 & (column == 1)
-    for slot, condition in (
-        ((1, 1), has_low),
-        ((1, 3), has_high),
-        ((1, 0), far_low),
-        ((1, 4), far_high),
-    ):
+    for slot, condition in (((1, 0), far_low), ((1, 4), far_high)):
         for half in (0, 1):
             landed(slot, half, condition)
         absorb_if(slot, condition)

time: 53.2 us -> 52.8 us (level)
  no operation moved by 1% of the time
where the time goes in v3:
time: 52.8 us; the launch traced here: 52.6 us
  Pallas kernels  50.9 us (96%)
  local copies, waits for them, and re-layouts  1.72 us (3%)
    pallas_call x1, Pallas kernels, per_device(): pl.pallas_call(functools.partial(kernel, n_seq, n_tp, capacity, inside),...  50.9 us
    unnamed x1, local copies, waits for them, and re-layouts  1.72 us

profile of v3, /device:TPU:0, one launch (start us, length us, event | category | flops | bytes accessed | tf_op | source)
XLA Modules:
  0.0 52.6 jit_solution(18048214961507587754)
XLA Ops:
  0.0 50.9 %shard_map.109 = bf16[8,16,1280]{2,1,0:T(8,128)(2,1)} custom-call(bf16[256,1280]{1,0:T(8,128)(2,1)} %tokens_hbm.1, f32[1280]{0:T(1024)} %gain_ref.1, f32[1280]{0:T(1024)} %bias_ref.1, bf16[3,320,1280]{2,1,0:T(8,128)(2,1)} %bitcast.4, f32[3,320]{1,0:T(4,128)} %b_qkv_ref.1, bf16[320,1280]{1,0:T(8,128)(2,1)} %w_out_hbm.1, f32[1280]{0:T(1024)} %b_out_ref.1, ...), custom_call_target="tpu_custom_call" | custom-call | flops 2000000000 | bytes 5000000 | tf_op jit(solution)/shard_map/pallas_call | solution.py:438
  50.9 1.7 %copy.13 = bf16[128,1280]{1,0:T(8,128)(2,1)} copy(bf16[128,1280]{1,0:T(8,128)(2,1)} %bitcast.3) | data formatting | bytes 655360

commit v4 on v3

--- a/solution.py
+++ b/solution.py
@@ -235,21 +235,21 @@
         return 2 * (pair + slot[1] - 2) + (column if slot[0] == 0 else 1 - column)
 
     def absorb(slots, first=False):
-        allowed = [own_segment == segment_row(block_of(slot)) for slot in slots]
+        allowed = [
+            jnp.where(own_segment == segment_row(block_of(slot)), 0.0, masked_score)
+            for slot in slots
+        ]
         for h in range(heads):
             lanes = slice(h * HEAD_DIM, (h + 1) * HEAD_DIM)
             query = query_ref[:, lanes]
             scores = [
-                jnp.where(
-                    mask,
-                    lax.dot_general(
-                        query,
-                        kv[slot[0], slot[1], 0, :, lanes],
-                        (((1,), (1,)), ((), ())),
-                        preferred_element_type=jnp.float32,
-                    ),
-                    masked_score,
+                lax.dot_general(
+                    query,
+                    kv[slot[0], slot[1], 0, :, lanes],
+                    (((1,), (1,)), ((), ())),
+                    preferred_element_type=jnp.float32,
                 )
+                + mask
                 for slot, mask in zip(slots, allowed)
             ]
             top = jnp.max(functools.reduce(jnp.maximum, scores), axis=1, keepdims=True)

time: 52.8 us -> 52.8 us (level)
  no operation moved by 1% of the time
where the time goes in v4:
time: 52.8 us; the launch traced here: 52.6 us
  Pallas kernels  50.9 us (96%)
  local copies, waits for them, and re-layouts  1.72 us (3%)
    pallas_call x1, Pallas kernels, per_device(): pl.pallas_call(functools.partial(kernel, n_seq, n_tp, capacity, inside),...  50.9 us
    unnamed x1, local copies, waits for them, and re-layouts  1.72 us

profile of v4, /device:TPU:0, one launch (start us, length us, event | category | flops | bytes accessed | tf_op | source)
XLA Modules:
  0.0 52.6 jit_solution(3351931767977922565)
XLA Ops:
  0.0 50.9 %shard_map.109 = bf16[8,16,1280]{2,1,0:T(8,128)(2,1)} custom-call(bf16[256,1280]{1,0:T(8,128)(2,1)} %tokens_hbm.1, f32[1280]{0:T(1024)} %gain_ref.1, f32[1280]{0:T(1024)} %bias_ref.1, bf16[3,320,1280]{2,1,0:T(8,128)(2,1)} %bitcast.4, f32[3,320]{1,0:T(4,128)} %b_qkv_ref.1, bf16[320,1280]{1,0:T(8,128)(2,1)} %w_out_hbm.1, f32[1280]{0:T(1024)} %b_out_ref.1, ...), custom_call_target="tpu_custom_call" | custom-call | flops 2000000000 | bytes 5000000 | tf_op jit(solution)/shard_map/pallas_call | solution.py:438
  50.9 1.7 %copy.13 = bf16[128,1280]{1,0:T(8,128)(2,1)} copy(bf16[128,1280]{1,0:T(8,128)(2,1)} %bitcast.3) | data formatting | bytes 655360
